TPU v7x, 32 devices: a whole 2x2x4 slice. The times are simulated.
32 devices in a mesh: groups: 2 (over y), cells: 4 (over z), corners: 2 (over x), kern: 2 (over core).
Axes of the slice: x: 2, y: 2, z: 4, core: 2. Of those that a mesh axis runs over, the one named last changes fastest.
Arguments:
- theta: float32 [64, 128, 128], P(('groups', 'cells')), parts along dimension 0, may hold values from -8 to 8
- target: bfloat16 [16, 128, 128], P(('groups', 'cells')), parts along dimension 0, may hold values from 0 to 1
- kernels: float32 [2, 2, 24, 35, 35], P(None, 'corners', 'kern'), may hold values from -25.33743 to 25.33743
- dose: float32 [2], P('corners'), may hold values from 0.6 to 1
- inst_owner: int32 [128, 1], P(('groups', 'cells')), parts along dimension 0, may hold values from 0 to 3; in each aligned block of 16 rows (0 to 15, 16 to 31, ...) at most 8 rows name the same one
- inst_local: int32 [128], P(('groups', 'cells')), parts along dimension 0, may hold values from 0 to 7
- inst_shift: int32 [128], P(('groups', 'cells')), parts along dimension 0, may hold values from 0 to 127
Outputs:
- theta_out: float32 [64, 128, 128], P(('groups', 'cells'), ('corners', 'kern')), parts along dimension 0
There are 2 independent parts, one for each index of `groups`. A program takes and returns all parts, laid end to end along the dimension named above; an argument that names none is the same for every part. Nothing has to cross between parts.
Inputs may be any that keep to these rules, and one draw needn't show every extreme that they name: `inst_owner`: within the rows of one device (aligned blocks of 16 rows) no owner is named by more than 8 rows, and in some block one owner is named by exactly 8.
All inputs are finite; a program needn't handle non-finite values.
Results may differ from a plain program's by a relative error of at most 0.003.
Values may be sent and summed in bfloat16 or wider, within the bound.
A program may use at most 64 MiB of HBM per device.

v0:
```python
import math

import jax
import jax.numpy as jnp
from jax import lax
from jax.sharding import PartitionSpec as P

ITERS = 2


LR = 0.25
EPS = 1e-06
STEEP = 3.0


def tables(cell_size, freq_count):
    freqs = jnp.arange(freq_count, dtype=jnp.int32) - freq_count // 2
    pixels = jnp.arange(cell_size, dtype=jnp.int32)
    phase = (freqs[:, None] * pixels[None, :] % cell_size).astype(jnp.float32) * (
        2.0 * math.pi / cell_size
    )
    fwd_real = jnp.cos(phase)
    fwd_imag = -jnp.sin(phase)
    inv_real = fwd_real.T / cell_size
    inv_imag = -fwd_imag.T / cell_size
    return (fwd_real, fwd_imag, inv_real, inv_imag)


def spectrum(field, tabs):
    fwd_real, fwd_imag = (tabs[0], tabs[1])
    hp = lax.Precision.HIGHEST
    left_real = jnp.einsum("fx,txy->tfy", fwd_real, field, precision=hp)
    left_imag = jnp.einsum("fx,txy->tfy", fwd_imag, field, precision=hp)
    spec_real = jnp.einsum("tfy,gy->tfg", left_real, fwd_real, precision=hp) - jnp.einsum(
        "tfy,gy->tfg", left_imag, fwd_imag, precision=hp
    )
    spec_imag = jnp.einsum("tfy,gy->tfg", left_real, fwd_imag, precision=hp) + jnp.einsum(
        "tfy,gy->tfg", left_imag, fwd_real, precision=hp
    )
    return (spec_real, spec_imag)


def intensity(field, kern_real, kern_imag, tabs):
    inv_real, inv_imag = (tabs[2], tabs[3])
    hp = lax.Precision.HIGHEST
    spec_real, spec_imag = spectrum(field, tabs)

    def add_kernel(running, pair):
        resp_real = pair[0] * spec_real - pair[1] * spec_imag
        resp_imag = pair[0] * spec_imag + pair[1] * spec_real
        half_real = jnp.einsum("tfg,yg->tfy", resp_real, inv_real, precision=hp) - jnp.einsum(
            "tfg,yg->tfy", resp_imag, inv_imag, precision=hp
        )
        half_imag = jnp.einsum("tfg,yg->tfy", resp_real, inv_imag, precision=hp) + jnp.einsum(
            "tfg,yg->tfy", resp_imag, inv_real, precision=hp
        )
        near_real = jnp.einsum("xf,tfy->txy", inv_real, half_real, precision=hp) - jnp.einsum(
            "xf,tfy->txy", inv_imag, half_imag, precision=hp
        )
        near_imag = jnp.einsum("xf,tfy->txy", inv_real, half_imag, precision=hp) + jnp.einsum(
            "xf,tfy->txy", inv_imag, half_real, precision=hp
        )
        return (running + near_real * near_real + near_imag * near_imag, None)

    start = jnp.zeros(field.shape, jnp.float32)
    result, unused = lax.scan(add_kernel, start, (kern_real, kern_imag))
    return result


def per_device(theta, target, kernels, dose, inst_owner, inst_local, inst_shift):
    hp = lax.Precision.HIGHEST
    n_owners = lax.axis_size("cells")
    members = lax.axis_size(("corners", "kern"))
    member = lax.axis_index(("corners", "kern"))
    cells_here = theta.shape[0]
    cell_size = theta.shape[1]
    inst_count = inst_local.shape[0]
    tile_count = target.shape[0]
    slot_count = inst_count // tile_count
    capacity = max(2, 2 * inst_count // n_owners)
    band_rows = cell_size // members
    tabs = tables(cell_size, kernels.shape[3])
    dose_now = dose[0]
    wanted = target.astype(jnp.float32)
    kern_real = kernels[0, 0]
    kern_imag = kernels[1, 0]
    owners = inst_owner[:, 0]
    inst_iota = jnp.arange(inst_count, dtype=jnp.int32)
    same_owner = (owners[None, :] == owners[:, None]) & (inst_iota[None, :] < inst_iota[:, None])
    rank_in = jnp.sum(same_owner.astype(jnp.int32), axis=1)
    slot_index = owners * capacity + rank_in
    slot_hit = slot_index[:, None] == jnp.arange(n_owners * capacity, dtype=jnp.int32)[None, :]
    used_slot = jnp.any(slot_hit, axis=0)
    asked_local = jnp.sum(jnp.where(slot_hit, inst_local[:, None], 0), axis=0)
    request = jnp.where(used_slot, asked_local, -1).reshape(n_owners, capacity)
    asked = lax.all_to_all(request, "cells", split_axis=0, concat_axis=0, tiled=True)
    picker = (
        asked.reshape(-1)[:, None] == jnp.arange(cells_here, dtype=jnp.int32)[None, :]
    ).astype(jnp.float32)
    picker_half = picker.astype(jnp.bfloat16)
    slot_weights = slot_hit.astype(jnp.float32)
    cell_params = lax.dynamic_slice_in_dim(theta, member * band_rows, band_rows, 1)
    rows_here = cell_params.shape[1]
    for iteration in range(ITERS):
        mask_vals = jax.nn.sigmoid(cell_params).astype(jnp.bfloat16)
        outgoing = jnp.dot(
            picker_half, mask_vals.reshape(cells_here, -1), preferred_element_type=jnp.float32
        )
        outgoing = outgoing.astype(jnp.bfloat16).reshape(n_owners, capacity, rows_here, cell_size)
        received = lax.all_to_all(outgoing, "cells", split_axis=0, concat_axis=0, tiled=True)
        placed = jnp.take(
            received.reshape(n_owners * capacity, rows_here, cell_size), slot_index, axis=0
        )
        transmit = 2.0 * placed.astype(jnp.float32) - 1.0
        rolled = jax.vmap(lambda plane, offset: jnp.roll(plane, offset, axis=1))(
            transmit, inst_shift
        )
        tile_part = (
            jnp.sum(rolled.reshape(tile_count, slot_count, rows_here, cell_size), axis=1)
            / slot_count
        )
        tile_field = lax.all_gather(tile_part, ("corners", "kern"), axis=1, tiled=True)
        partial_image, pullback = jax.vjp(
            lambda plane: intensity(plane, kern_real, kern_imag, tabs), tile_field
        )
        image = lax.psum(partial_image.astype(jnp.bfloat16), "kern").astype(jnp.float32)
        resist = jax.nn.sigmoid(STEEP * (dose_now * image - 1.0))
        pressure = 2.0 * (resist - wanted) * resist * (1.0 - resist) * STEEP * dose_now
        tile_grad = pullback(pressure)[0]
        grad_part = lax.psum_scatter(
            tile_grad.astype(jnp.bfloat16), ("corners", "kern"), scatter_dimension=1, tiled=True
        ).astype(jnp.float32)
        inst_grads = jnp.repeat(grad_part, slot_count, axis=0)
        unrolled = jax.vmap(lambda plane, offset: jnp.roll(plane, -offset, axis=1))(
            inst_grads, inst_shift
        )
        slot_grads = jnp.dot(slot_weights.T, unrolled.reshape(inst_count, -1), precision=hp)
        slot_grads = slot_grads.reshape(n_owners, capacity, rows_here, cell_size)
        returned = lax.all_to_all(slot_grads, "cells", split_axis=0, concat_axis=0, tiled=True)
        cell_sums = jnp.dot(picker.T, returned.reshape(n_owners * capacity, -1), precision=hp)
        cell_sums = cell_sums.reshape(cells_here, rows_here, cell_size)
        squash = jax.nn.sigmoid(cell_params)
        gradient = cell_sums * (2.0 / slot_count) * squash * (1.0 - squash)
        squares = jnp.sum(gradient * gradient, axis=(1, 2))
        squares = lax.psum(squares, ("corners", "kern"))
        cell_params = (
            cell_params
            - LR * gradient / jnp.sqrt(squares / (cell_size * cell_size) + EPS)[:, None, None]
        )
    return cell_params


def solution(mesh):
    in_specs = (
        P(("groups", "cells"), None, None),
        P(("groups", "cells"), None, None),
        P(None, "corners", "kern", None, None),
        P("corners"),
        P(("groups", "cells"), None),
        P(("groups", "cells")),
        P(("groups", "cells")),
    )
    out_specs = P(("groups", "cells"), ("corners", "kern"), None)
    return jax.shard_map(
        per_device, mesh=mesh, in_specs=in_specs, out_specs=out_specs, check_vma=False
    )
```

profile of v0, /device:TPU:0, one launch (start us, length us, event | category | flops | bytes accessed | tf_op | source)
XLA Modules:
  0.0 496.8 jit_solution(15146863222986831006)
XLA Ops:
  9.6 6.3 %all-to-all-start = ((s32[4,1,8]{2,1,0:T(1,128)}), s32[4,1,8]{2,1,0:T(1,128)S(1)}, u32[]{:S(2)}, u32[]{:S(2)}) async-start(s32[4,1,8]{2,1,0:T(1,128)} %bitcast.3), calls=%async_computation | async-start | bytes 4096 | tf_op jit(solution)/shard_map/all_to_all | solution.py:96
  18.4 3.1 all-to-all-done
  23.7 3.4 all-to-all-start.1
  27.9 6.2 %all-to-all-done.1 = bf16[4,8,32,128]{3,2,1,0:T(8,128)(2,1)S(1)} async-done(((bf16[4,8,32,128]{3,2,1,0:T(8,128)(2,1)}), bf16[4,8,32,128]{3,2,1,0:T(8,128)(2,1)S(1)}, u32[]{:S(2)}, u32[]{:S(2)}) %all-to-all-start.1) | async-done | bytes 262176 | tf_op jit(solution)/shard_map/all_to_all | solution.py:110
  34.9 1.3 copy.84
  36.2 3.0 gather_fusion.1
  39.2 1.6 bitcast_reduce_fusion.1
  40.9 5.4 %all_gather.6 = f32[2,128,128]{2,1,0:T(8,128)S(1)} all-gather(f32[2,32,128]{2,1,0:T(8,128)S(1)} %broadcast_multiply_fusion.1), channel_id=1, replica_groups=mesh['groups'=2,'cells'=4,'corners'=2,'kern'=2] {'corners','kern'}, dimensions={1}, use_global_device_ids=true | all-gather | bytes 163840 | tf_op jit(solution)/shard_map/all_gather | solution.py:122
  48.3 1.3 broadcast.159.clone
  49.8 63.0 %while.92 = (s32[]{:T(128)}, f32[2,128,128]{1,2,0:T(8,128)S(1)}, f32[12,1,35,35]{3,2,1,0:T(8,128)S(1)}, f32[12,1,35,35]{3,2,1,0:T(8,128)S(1)}, f32[12,2,128,128]...) while((s32[]{:T(128)}, f32[2,128,128]{1,2,0:T(8,128)S(1)}, ...), condition=%wide.region_5.8_spmd.clone.clone.clone.clone, body=%wide.region_4.7_spmd.clone.clone.clone.clone.sunk | while | flops 70917336 | bytes 2136583 | solution.py:66
  114.6 16.4 %all-reduce.8.cloned.1.call-done = bf16[2,128,128]{1,2,0:T(8,128)(2,1)} async-done(((bf16[2,128,128]{1,2,0:T(8,128)(2,1)}), bf16[2,128,128]{1,2,0:T(8,128)(2,1)}) %all-reduce.8.cloned.1.call-update) | async-done | bytes 65552 | tf_op jit(solution)/shard_map/psum | solution.py:126
  131.9 56.9 %while.93 = (s32[]{:T(128)}, f32[2,35,35]{2,1,0:T(8,128)S(1)}, f32[2,35,35]{2,1,0:T(8,128)S(1)}, f32[12,1,35,35]{3,2,1,0:T(8,128)S(1)}, f32[12,2,128,128]{2,3,1,...) while((s32[]{:T(128)}, f32[2,35,35]{2,1,0:T(8,128)S(1)}, ...), condition=%wide.region_8.11_spmd.clone.clone.clone.clone, body=%wide.region_7.10_spmd.clone.clone.clone.clone.sunk | while | flops 70994280 | bytes 1536399 | solution.py:66
  132.3 1.3 fusion.691
  134.3 1.3 fusion.694
  137.1 1.3 fusion.691
  139.1 1.3 fusion.694
  141.8 1.3 fusion.691
  143.8 1.3 fusion.694
  146.6 1.3 fusion.691
  148.6 1.3 fusion.694
  151.3 1.3 fusion.691
  153.3 1.3 fusion.694
  156.0 1.3 fusion.691
  158.1 1.3 fusion.694
  162.8 1.3 fusion.694
  167.5 1.3 fusion.694
  172.3 1.3 fusion.694
  177.0 1.3 fusion.694
  181.8 1.3 fusion.694
  186.5 1.3 fusion.694
  193.1 31.1 %all-reduce.12.cloned.1.call-done = bf16[2,128,128]{2,0,1:T(2,128)(2,1)} async-done(((bf16[2,128,128]{2,0,1:T(2,128)(2,1)}), bf16[2,128,128]{2,0,1:T(2,128)(2,1)}) %all-reduce.12.cloned.1.call-update) | async-done | bytes 65552
  225.0 1.3 copy.90
  226.3 3.0 gather_fusion.2
  229.3 1.6 copy.91
  231.5 17.9 %all_to_all.26 = f32[4,8,32,128]{3,1,2,0:T(8,128)S(1)} all-to-all(f32[4,8,32,128]{3,1,2,0:T(8,128)S(1)} %fusion.356), channel_id=1, replica_groups=mesh['groups'=2,'cells'=4,'corners'=2,'kern'=2] {'cells'}, dimensions={0} | all-to-all | bytes 1048576 | tf_op jit(solution)/shard_map/all_to_all | solution.py:139
  249.8 5.7 %psum.29 = f32[8]{0:T(128)S(1)} all-reduce(f32[8]{0:T(128)S(1)} %get-tuple-element.1373), channel_id=1, replica_groups=mesh['groups'=2,'cells'=4,'corners'=2,'kern'=2] {'corners','kern'}, use_global_device_ids=true, to_apply=%region_11.14 | all-reduce | flops 8 | bytes 64 | tf_op jit(solution)/shard_map/psum | solution.py:145
  256.6 3.4 all-to-all-start.3
  260.1 9.1 %all-to-all-done.3 = bf16[4,8,32,128]{3,2,1,0:T(8,128)(2,1)S(1)} async-done(((bf16[4,8,32,128]{3,2,1,0:T(8,128)(2,1)}), bf16[4,8,32,128]{3,2,1,0:T(8,128)(2,1)S(1)}, u32[]{:S(2)}, u32[]{:S(2)}) %all-to-all-start.3) | async-done | bytes 262176 | tf_op jit(solution)/shard_map/all_to_all | solution.py:110
  269.9 1.3 copy.95
  271.2 3.0 gather_fusion.4
  274.2 1.6 bitcast_reduce_fusion
  275.9 5.6 %all_gather.7 = f32[2,128,128]{2,1,0:T(8,128)S(1)} all-gather(f32[2,32,128]{2,1,0:T(8,128)S(1)} %broadcast_multiply_fusion), channel_id=1, replica_groups=mesh['groups'=2,'cells'=4,'corners'=2,'kern'=2] {'corners','kern'}, dimensions={1}, use_global_device_ids=true | all-gather | bytes 163840 | tf_op jit(solution)/shard_map/all_gather | solution.py:122
  283.5 1.3 broadcast.159
  285.1 63.0 %while.94 = (s32[]{:T(128)}, f32[2,128,128]{1,2,0:T(8,128)S(1)}, f32[12,1,35,35]{3,2,1,0:T(8,128)S(1)}, f32[12,1,35,35]{3,2,1,0:T(8,128)S(1)}, f32[12,2,128,128]...) while((s32[]{:T(128)}, f32[2,128,128]{1,2,0:T(8,128)S(1)}, ...), condition=%wide.region_14.17_spmd.clone.clone.clone.clone, body=%wide.region_13.16_spmd.clone.clone.clone.clone.sunk | while | flops 70917336 | bytes 2136583 | solution.py:66
  348.9 16.2 %all-reduce.10.cloned.1.call-done = bf16[2,128,128]{1,2,0:T(8,128)(2,1)} async-done(((bf16[2,128,128]{1,2,0:T(8,128)(2,1)}), bf16[2,128,128]{1,2,0:T(8,128)(2,1)}) %all-reduce.10.cloned.1.call-update) | async-done | bytes 65552 | tf_op jit(solution)/shard_map/psum | solution.py:126
  366.0 56.9 %while.95 = (s32[]{:T(128)}, f32[2,35,35]{2,1,0:T(8,128)S(1)}, f32[2,35,35]{2,1,0:T(8,128)S(1)}, f32[12,1,35,35]{3,2,1,0:T(8,128)S(1)}, f32[12,2,128,128]{2,3,1,...) while((s32[]{:T(128)}, f32[2,35,35]{2,1,0:T(8,128)S(1)}, ...), condition=%wide.region_17.20_spmd.clone.clone.clone.clone, body=%wide.region_16.19_spmd.clone.clone.clone.clone.sunk | while | flops 70994280 | bytes 1536399 | solution.py:66
  368.4 1.3 fusion.731
  373.1 1.3 fusion.731
  377.9 1.3 fusion.731
  382.6 1.3 fusion.731
  387.4 1.3 fusion.731
  392.1 1.3 fusion.731
  396.8 1.3 fusion.731
  401.6 1.3 fusion.731
  406.3 1.3 fusion.731
  411.1 1.3 fusion.731
  415.8 1.3 fusion.731
  420.5 1.3 fusion.731
  425.9 32.4 %all-reduce.14.cloned.1.call-done = bf16[2,128,128]{2,0,1:T(2,128)(2,1)} async-done(((bf16[2,128,128]{2,0,1:T(2,128)(2,1)}), bf16[2,128,128]{2,0,1:T(2,128)(2,1)}) %all-reduce.14.cloned.1.call-update) | async-done | bytes 65552
  459.0 1.3 copy.99
  460.3 3.0 gather_fusion.5
  463.3 1.6 copy.100
  465.5 17.9 %all_to_all.27 = f32[4,8,32,128]{3,1,2,0:T(8,128)S(1)} all-to-all(f32[4,8,32,128]{3,1,2,0:T(8,128)S(1)} %fusion.354), channel_id=1, replica_groups=mesh['groups'=2,'cells'=4,'corners'=2,'kern'=2] {'cells'}, dimensions={0} | all-to-all | bytes 1048576 | tf_op jit(solution)/shard_map/all_to_all | solution.py:139
  483.8 5.7 %psum.31 = f32[8]{0:T(128)S(1)} all-reduce(f32[8]{0:T(128)S(1)} %get-tuple-element.1375), channel_id=1, replica_groups=mesh['groups'=2,'cells'=4,'corners'=2,'kern'=2] {'corners','kern'}, use_global_device_ids=true, to_apply=%region_20.23 | all-reduce | flops 8 | bytes 64 | tf_op jit(solution)/shard_map/psum | solution.py:145
  (568 shorter events, 227.0 us)
Async XLA Ops:
  6.5 11.8 %copy-start = (f32[8,128,128]{2,1,0:T(8,128)S(1)}, f32[8,128,128]{2,1,0:T(8,128)}, u32[]{:S(2)}) copy-start(f32[8,128,128]{2,1,0:T(8,128)} %param.19) | copy-start | bytes 1572868
  9.6 11.9 %all-to-all-start = ((s32[4,1,8]{2,1,0:T(1,128)}), s32[4,1,8]{2,1,0:T(1,128)S(1)}, u32[]{:S(2)}, u32[]{:S(2)}) async-start(s32[4,1,8]{2,1,0:T(1,128)} %bitcast.3), calls=%async_computation | async-start | bytes 4096 | tf_op jit(solution)/shard_map/all_to_all | solution.py:96
  18.4 8.8 %copy-start.3 = (f32[8,32,128]{2,1,0:T(8,128)}, f32[8,32,128]{2,1,0:T(8,128)S(1)}, u32[]{:S(2)}) copy-start(f32[8,32,128]{2,1,0:T(8,128)S(1)} %constant_dynamic-slice_fusion.2) | copy-start | bytes 393220
  23.7 10.5 %all-to-all-start.1 = ((bf16[4,8,32,128]{3,2,1,0:T(8,128)(2,1)}), bf16[4,8,32,128]{3,2,1,0:T(8,128)(2,1)S(1)}, u32[]{:S(2)}, u32[]{:S(2)}) async-start(bf16[4,8,32,128]{3,2,1,0:T(8,128)(2,1)} %copy.83), calls=%async_computation.1 | async-start | bytes 524288 | tf_op jit(solution)/shard_map/all_to_all | solution.py:110
  27.1 103.9 %all-reduce.8.cloned.1.call-start = ((), (), s32[]{:S(2)}) async-start(), calls=%async_computation.5 | async-start | bytes 131072 | tf_op jit(solution)/shard_map/psum | solution.py:126
  49.8 64.6 %copy-start.7 = (bf16[2,128,128]{2,1,0:T(8,128)(2,1)S(1)}, bf16[2,128,128]{2,1,0:T(8,128)(2,1)}, u32[]{:S(2)}) copy-start(bf16[2,128,128]{2,1,0:T(8,128)(2,1)} %param.20) | copy-start | bytes 196612
  113.5 110.7 %all-reduce.12.cloned.1.call-start = ((), (), s32[]{:S(2)}) async-start(), calls=%async_computation.7 | async-start | bytes 131072
  114.6 17.4 %copy-start.1 = (bf16[2,128,128]{1,2,0:T(8,128)(2,1)}, bf16[2,128,128]{1,2,0:T(8,128)(2,1)S(1)}, u32[]{:S(2)}) copy-start(bf16[2,128,128]{1,2,0:T(8,128)(2,1)S(1)} %copy.87) | copy-start | bytes 196612
  131.9 59.9 %copy-start.8 = (u32[32]{0:T(128)S(1)}, u32[32]{0:T(128)}, u32[]{:S(2)}) copy-start(u32[32]{0:T(128)} %constant.353) | copy-start | bytes 388
  229.3 20.0 %copy-start.4 = (f32[8,32,128]{2,1,0:T(8,128)S(1)}, f32[8,32,128]{2,1,0:T(8,128)}, u32[]{:S(2)}) copy-start(f32[8,32,128]{2,1,0:T(8,128)} %copy-done.3) | copy-start | bytes 393220
  255.6 14.3 %copy-start.5 = (f32[8,32,128]{2,0,1:T(8,128)}, f32[8,32,128]{2,0,1:T(8,128)S(1)}, u32[]{:S(2)}) copy-start(f32[8,32,128]{2,0,1:T(8,128)S(1)} %divide_subtract_fusion.1) | copy-start | bytes 393220
  256.6 12.6 %all-to-all-start.3 = ((bf16[4,8,32,128]{3,2,1,0:T(8,128)(2,1)}), bf16[4,8,32,128]{3,2,1,0:T(8,128)(2,1)S(1)}, u32[]{:S(2)}, u32[]{:S(2)}) async-start(bf16[4,8,32,128]{3,2,1,0:T(8,128)(2,1)} %copy.94), calls=%async_computation.3 | async-start | bytes 524288 | tf_op jit(solution)/shard_map/all_to_all | solution.py:110
  260.0 105.1 %all-reduce.10.cloned.1.call-start = ((), (), s32[]{:S(2)}) async-start(), calls=%async_computation.6 | async-start | bytes 131072 | tf_op jit(solution)/shard_map/psum | solution.py:126
  285.1 80.0 %copy-start.2 = (bf16[2,128,128]{1,2,0:T(8,128)(2,1)S(1)}, bf16[2,128,128]{1,2,0:T(8,128)(2,1)}, u32[]{:S(2)}) copy-start(bf16[2,128,128]{1,2,0:T(8,128)(2,1)} %copy-done.1) | copy-start | bytes 196612
  348.8 109.4 %all-reduce.14.cloned.1.call-start = ((), (), s32[]{:S(2)}) async-start(), calls=%async_computation.8 | async-start | bytes 131072
  463.3 20.0 %copy-start.6 = (f32[8,32,128]{2,0,1:T(8,128)S(1)}, f32[8,32,128]{2,0,1:T(8,128)}, u32[]{:S(2)}) copy-start(f32[8,32,128]{2,0,1:T(8,128)} %copy-done.5) | copy-start | bytes 393220
Sparse Core Ops, SparseCore 0:
  113.6 17.3 all-reduce.7
  191.9 32.2 all-reduce.11
  348.9 16.0 all-reduce.9
  426.0 32.2 all-reduce.13
where the time goes:
time: 501 us; the launch traced here: 497 us
  matrix products  211 us (42%)
  waiting for transfers between devices  115 us (23%)
  local copies, waits for them, and re-layouts  69.9 us (14%)
  blocking collectives  58.2 us (12%)
  between operations  15.1 us (3%)
  starting transfers between devices  13.5 us (3%)
  other arithmetic  11.2 us (2%)
    unnamed x6, waiting for transfers between devices  63.5 us
    dot_general x48, matrix products, add_kernel(): jnp.einsum('xf,tfy->txy', inv_imag, half_imag, precision=hp)  57.2 us
    dot_general x48, matrix products, add_kernel(): jnp.einsum('xf,tfy->txy', inv_real, half_real, precision=hp)  41.5 us
    all_to_all x2, blocking collectives, per_device(): lax.all_to_all(slot_grads, 'cells', split_axis=0, concat_axis=0, tiled=True)  35.8 us
    psum x2, waiting for transfers between devices, per_device(): lax.psum(partial_image.astype(jnp.bfloat16), 'kern').astype(jnp.float32)  32.6 us
    dot_general x48, matrix products, add_kernel(): jnp.einsum('xf,tfy->txy', inv_imag, half_real, precision=hp)  19.8 us
    dot_general x48, matrix products, add_kernel(): jnp.einsum('xf,tfy->txy', inv_real, half_imag, precision=hp)  19.5 us
    dynamic_update_slice x48, local copies, waits for them, and re-layouts, intensity(): result, unused = lax.scan(add_kernel, start, (kern_real, kern_imag))  18.1 us
  transfers between devices with their start and end apart: 7, of which 7 were waited for; matrix products, arithmetic and copies ran while one was open for 1% of the time, Pallas kernels for 0%

commit v1 on v0

v1 whole, which is shorter than its diff:
```python
import functools
import math

import jax
import jax.numpy as jnp
import numpy as np
from jax import lax
from jax.experimental import pallas as pl
from jax.experimental.pallas import tpu as pltpu
from jax.sharding import PartitionSpec as P

ITERS = 2
LR = 0.25
EPS = 1e-06
STEEP = 3.0
MESH = pl.DeviceIdType.MESH
HALF = jnp.bfloat16
LINK = jnp.bfloat16


def round_up(value, step):
    return -(-value // step) * step


def layout(count, lanes):
    half = count // 2 + 1
    blocks = max(1, lanes // (2 * half))
    share = -(-count // blocks)
    return half, blocks, share, round_up(share, 16)


def tables(size, count, mid):
    lanes = 2 * mid
    half, blocks, share, tall = layout(count, lanes)
    rows = blocks * tall
    centre = count // 2
    row_of = np.array([f // share * tall + f % share for f in range(count)])

    def placed(matrix):
        result = np.zeros((rows,) + matrix.shape[1:])
        result[row_of] = matrix
        return result

    freqs = np.arange(count) - centre
    phase = (freqs[:, None] * np.arange(size)[None, :] % size) * (2.0 * math.pi / size)
    cos, sin = np.cos(phase), -np.sin(phase)
    fr, fi = placed(cos), placed(sin)
    lr = np.zeros((mid, size))
    li = np.zeros((mid, size))
    lr[:count], li[:count] = cos, sin
    fy = np.zeros((size, lanes))
    fyi = np.zeros((lanes, 2 * size))
    keep = np.zeros((lanes, lanes))
    turned = np.zeros((lanes, lanes))
    for b in range(blocks):
        for g in range(half):
            re = b * 2 * half + g
            im = re + half
            fy[:, re], fy[:, im] = cos[centre + g], sin[centre + g]
            fyi[re] = np.concatenate([cos[centre + g], -sin[centre + g]])
            fyi[im] = np.concatenate([sin[centre + g], cos[centre + g]])
            keep[re, centre + g] = keep[im, mid + centre + g] = 1.0
            if g > 0:
                turned[re, centre - g], turned[im, mid + centre - g] = 1.0, -1.0
    fl = np.concatenate([fr, fi], 0)
    flip = np.zeros((rows, rows))
    flip[row_of, row_of[::-1]] = 1.0
    expand = np.concatenate([keep, turned], 0)
    fold = np.concatenate([keep.T, turned.T], 0)
    flt = fl.T
    gy = np.block([[lr, -li], [li, lr]]) / size
    grid = min(size, round_up(2 * count - 1, 8))
    turn = (freqs[:, None] * np.arange(grid)[None, :] % grid) * (2.0 * math.pi / grid)
    sr, si = placed(np.cos(turn)), placed(-np.sin(turn))
    gl = np.block([[sr.T, si.T], [-si.T, sr.T]]) / size
    gap = np.arange(size)[:, None] / size - np.arange(grid)[None, :] / grid
    band = np.arange(-2 * (count // 2), 2 * (count // 2) + 1)
    wide = np.cos(2.0 * math.pi * band[:, None, None] * gap[None]).sum(0) / grid
    if grid == size:
        wide = np.eye(size)
    parts = dict(fy=fy, fl=fl, fyi=fyi, flt=flt, gy=gy, gyt=gy.T, gl=gl, glt=gl.T, wt=wide.T, flip=flip, expand=expand, fold=fold)
    places, stack, top = {}, [], 0
    for name, t in parts.items():
        places[name] = []
        for left in range(0, t.shape[1], 128):
            piece = t[:, left : left + 128]
            tall = round_up(piece.shape[0], 16)
            places[name].append((top, *piece.shape))
            padded = np.zeros((tall, 128), np.float32)
            padded[: piece.shape[0], : piece.shape[1]] = piece
            stack.append(padded)
            top += tall
    return places, np.concatenate(stack, 0).astype(HALF), wide.astype(np.float32), grid


def dot(a, b):
    return jnp.dot(a.astype(HALF), b.astype(HALF), preferred_element_type=jnp.float32)


def body(sizes, places, theta_hbm, target_hbm, kernels_hbm, dose, owner, local, shift, tabs_hbm, wide_hbm, out,
         theta, target, kernels, tabs, wide, loads, params, wsend, wrecv, kin, krr, kii, near, spectra, psend, precv, gsend, grecv,
         ws, wr, ks, kr, ps, pr, gs, gr):
    n_z, n_x, n_k, count, grid = sizes
    cells, size = theta.shape[0], theta.shape[1]
    slots = local.shape[0] // target.shape[0]
    here = kernels.shape[0] // (2 * count)
    rows, lanes = krr.shape[1], krr.shape[2]
    mid = lanes // 2
    half, blocks, share, tall = layout(count, lanes)
    z, x, k = lax.axis_index("cells"), lax.axis_index("corners"), lax.axis_index("kern")
    zk = [(a, b) for a in range(n_z) for b in range(n_k) if (a, b) != (0, 0)]
    others = [(a, c, b) for a in range(n_z) for c in range(n_x) for b in range(n_k) if (a, c, b) != (0, 0, 0)]

    def at(a, b, c=0):
        return {"cells": lax.rem(z + a, n_z), "corners": lax.rem(x + c, n_x), "kern": lax.rem(k + b, n_k)}

    def send(src, dst, s, r, device):
        copy = pltpu.make_async_remote_copy(
            src_ref=src, dst_ref=dst, send_sem=s, recv_sem=r, device_id=device, device_id_type=MESH
        )
        copy.start()
        return copy

    def table(name):
        pieces = [tabs[top : top + tall, :across] for top, tall, across in places[name]]
        return pieces[0] if len(pieces) == 1 else jnp.concatenate(pieces, 1)

    local_copies = []
    pairs = [(theta_hbm, theta), (tabs_hbm, tabs), (kernels_hbm, kernels), (target_hbm, target), (wide_hbm, wide)]
    for j, (src, dst) in enumerate(pairs):
        copy = pltpu.make_async_copy(src, dst, loads.at[j])
        copy.start()
        local_copies.append(copy)
    barrier = pltpu.get_barrier_semaphore()
    for a, c, b in others:
        pl.semaphore_signal(barrier, inc=1, device_id=at(a, b, c), device_id_type=MESH)

    lane = lax.broadcasted_iota(jnp.int32, (slots, lanes), 1)
    row = lax.broadcasted_iota(jnp.int32, (slots, lanes), 0)
    freq = lane % half
    used = lane < 2 * half * blocks
    offsets = jnp.zeros((slots, lanes), jnp.int32)
    ids = []
    for j in range(slots):
        at_inst = k * slots + j
        offsets = jnp.where(row == j, shift[at_inst], offsets)
        ids.append(owner[at_inst] * cells + local[at_inst])
    turn = lax.rem(freq * offsets, size).astype(jnp.float32) * (2.0 * math.pi / size)
    phr = jnp.where(used, jnp.cos(turn), 0.0) / slots
    phi = jnp.where(used, -jnp.sin(turn), 0.0) / slots
    every = lax.broadcasted_iota(jnp.int32, (n_z * cells, lanes), 0)
    wrr = jnp.zeros((n_z * cells, lanes), jnp.float32)
    wii = jnp.zeros((n_z * cells, lanes), jnp.float32)
    for j in range(slots):
        hit = every == ids[j]
        wrr += jnp.where(hit, phr[j : j + 1], 0.0)
        wii += jnp.where(hit, phi[j : j + 1], 0.0)
    wsend[:, :, :lanes] = wrr.reshape(n_z, cells, lanes)
    wsend[:, :, lanes:] = wii.reshape(n_z, cells, lanes)

    pl.semaphore_wait(barrier, len(others))
    flying = []
    wcopies, kcopies = [], []
    for a, b in zk:
        wcopies.append(send(wsend.at[lax.rem(z + a, n_z)], wrecv.at[a, b], ws.at[a, b], wr.at[a, b], at(a, b)))
    for b in range(1, n_k):
        kcopies.append(send(kernels_hbm, kin.at[b], ks.at[b], kr.at[b], at(0, b)))
    wrecv[0, 0] = wsend[z]
    flying += wcopies + kcopies

    lane = lax.broadcasted_iota(jnp.int32, (rows, lanes), 1)
    sign = jnp.where(lane < mid, -1.0, 1.0)
    lane = lane[:tall]
    block = lane // (2 * half)
    is_real = lane % (2 * half) < half

    def times_i(value):
        return sign * pltpu.roll(value, mid, 1)

    def packed_times_i(value):
        return jnp.where(is_real, -pltpu.roll(value, lanes - half, 1), pltpu.roll(value, half, 1))

    def gather_blocks(value):
        result = value[:tall]
        for b in range(1, blocks):
            result = jnp.where(block == b, value[b * tall : (b + 1) * tall], result)
        return result

    def part_blocks(value):
        return jnp.concatenate([jnp.where(block == b, value, 0.0) for b in range(blocks)], 0)

    first_lane = lax.broadcasted_iota(jnp.int32, (size, lanes), 1)
    centre = jnp.where((first_lane % (2 * half) == 0) & (first_lane < 2 * half * blocks), float(size), 0.0)

    def cell_spectra(source):
        for c in range(cells):
            mask = jax.nn.sigmoid(source[c]).astype(HALF)
            right = 2.0 * dot(mask, table("fy")) - centre
            both = dot(table("fl"), right)
            spectra[c] = gather_blocks(both[:rows]) + packed_times_i(gather_blocks(both[rows:]))

    def spread(source, base):
        for part, wider in ((0, krr), (1, kii)):
            for j in range(here):
                first = (part * here + j) * count
                wider[base + j] = jnp.zeros((rows, lanes), jnp.float32)
                for b in range(blocks):
                    many = min(share, count - b * share)
                    wider[base + j, b * tall : b * tall + many, :count] = (
                        source[first + b * share : first + b * share + many]
                    )
                value = wider[base + j]
                wider[base + j] = value + pltpu.roll(value, mid, 1)

    for copy in local_copies[:2]:
        copy.wait()
    cell_spectra(theta)
    for copy in local_copies[2:]:
        copy.wait()
    spread(kernels, 0)
    for copy in wcopies:
        copy.wait_recv()

    chunk = math.gcd(12, here * n_k)
    steps = here * n_k // chunk
    wanted = target[k].astype(jnp.float32)
    dose_now = dose[0]

    for it in range(ITERS):
        source = theta if it == 0 else params
        if it > 0:
            cell_spectra(source)
        totals = [jnp.zeros((tall, lanes), jnp.float32) for a in range(n_z)]
        for c in range(cells):
            value = spectra[c]
            turned = packed_times_i(value)
            for a in range(n_z):
                w = wrecv[a, 0, c : c + 1]
                totals[a] += w[:, :lanes] * value + w[:, lanes:] * turned
        pcopies = []
        for a in range(1, n_z):
            psend[it, a] = totals[a].astype(LINK)
            pcopies.append(send(psend.at[it, a], precv.at[it, a], ps.at[it, a], pr.at[it, a],
                                {"cells": lax.rem(z - a + n_z, n_z)}))
        flying += pcopies
        spec = totals[0]
        if it == 0:
            for b, copy in zip(range(1, n_k), kcopies):
                copy.wait_recv()
                spread(kin.at[b], b * here)
        for a in range(1, n_z):
            pcopies[a - 1].wait_recv()
            spec += precv[it, a].astype(jnp.float32)
        spec = part_blocks(spec).astype(HALF)
        spec = dot(jnp.concatenate([spec, dot(table("flip"), spec).astype(HALF)], 1), table("expand"))
        turned_spec = times_i(spec)

        def forward(step, image):
            resp = []
            for j in range(chunk):
                at_k = step * chunk + j
                resp.append((krr[at_k] * spec + kii[at_k] * turned_spec).astype(HALF))
            half = dot(jnp.concatenate(resp, 0), table("gy")).astype(HALF)
            for j in range(chunk):
                one = half[j * rows : (j + 1) * rows]
                stacked = jnp.concatenate([one[:, :size], one[:, size:]], 0)
                both = dot(table("gl"), stacked)
                near[step * chunk + j] = both.astype(HALF)
                image += both[:grid] * both[:grid] + both[grid:] * both[grid:]
            return image

        image = lax.fori_loop(0, steps, forward, jnp.zeros((grid, size), jnp.float32))
        image = jnp.dot(wide[...], image, precision=lax.Precision.HIGHEST, preferred_element_type=jnp.float32)
        resist = jax.nn.sigmoid(STEEP * (dose_now * image - 1.0))
        pressure = (4.0 * STEEP) * dose_now * (resist - wanted) * resist * (1.0 - resist)
        pressure = dot(table("wt"), pressure)
        pressure = jnp.concatenate([pressure, pressure], 0)

        def backward(step, sums):
            first, second = sums
            halves = []
            for j in range(chunk):
                both = near[step * chunk + j].astype(jnp.float32) * pressure
                left = dot(table("glt"), both).astype(HALF)
                halves.append(jnp.concatenate([left[:rows], left[rows:]], 1))
            right = dot(jnp.concatenate(halves, 0), table("gyt"))
            for j in range(chunk):
                at_k = step * chunk + j
                one = right[j * rows : (j + 1) * rows]
                first += krr[at_k] * one
                second += kii[at_k] * one
            return first, second

        zero = jnp.zeros((rows, lanes), jnp.float32)
        first, second = lax.fori_loop(0, steps, backward, (zero, zero))
        tile = first - times_i(second)
        tile = tile.astype(HALF)
        tile = dot(jnp.concatenate([tile, dot(table("flip"), tile).astype(HALF)], 1), table("fold"))
        tile = gather_blocks(tile)
        gsend[it] = tile.astype(LINK)
        gcopies = {}
        for a, c, b in others:
            gcopies[a, c, b] = send(gsend.at[it], grecv.at[it, a, c, b], gs.at[it, a, c, b], gr.at[it, a, c, b], at(a, b, c))
        flying += list(gcopies.values())
        sums = [jnp.zeros((tall, lanes), jnp.float32) for c in range(cells)]
        for a, b in [(0, 0)] + zk:
            for c in range(n_x):
                if (a, c, b) != (0, 0, 0):
                    gcopies[a, c, b].wait_recv()
                    part = grecv[it, a, c, b].astype(jnp.float32)
                    tile = part if c == 0 else tile + part
            turned = packed_times_i(tile)
            for c in range(cells):
                w = wrecv[a, b, c : c + 1]
                sums[c] += w[:, :lanes] * tile - w[:, lanes:] * turned
        right = dot(jnp.concatenate([part_blocks(one) for one in sums], 0), table("fyi")).astype(HALF)
        for c in range(cells):
            one = right[c * rows : (c + 1) * rows]
            plane = dot(table("flt"), jnp.concatenate([one[:, :size], one[:, size:]], 0))
            now = source[c]
            squash = jax.nn.sigmoid(now)
            grad = 2.0 * plane * squash * (1.0 - squash)
            square = jnp.sum(jnp.sum(grad * grad, axis=0, keepdims=True), axis=1, keepdims=True)
            params[c] = now - grad * (LR * lax.rsqrt(square / (size * size) + EPS))
    band = out.shape[1]
    start = pl.multiple_of((x * n_k + k) * band, band)
    out[...] = params[:, pl.ds(start, band), :]
    for copy in flying:
        copy.wait_send()


def per_device(theta, target, kernels, dose, inst_owner, inst_local, inst_shift):
    n_z, n_x, n_k = lax.axis_size("cells"), lax.axis_size("corners"), lax.axis_size("kern")
    cells, size = theta.shape[0], theta.shape[1]
    count = kernels.shape[3]
    here = kernels.shape[2]
    assert target.shape[0] == n_k
    mid = round_up(count, 64)
    lanes = 2 * mid
    half, blocks, share, tall = layout(count, lanes)
    rows = blocks * tall
    places, tabs, wide, grid = tables(size, count, mid)
    kernels = kernels.reshape(2 * here * count, count)
    f32, dma = jnp.float32, pltpu.SemaphoreType.DMA
    hbm = pl.BlockSpec(memory_space=pltpu.HBM)
    vmem, smem = pl.BlockSpec(memory_space=pltpu.VMEM), pl.BlockSpec(memory_space=pltpu.SMEM)
    return pl.pallas_call(
        functools.partial(body, (n_z, n_x, n_k, count, grid), places),
        out_shape=jax.ShapeDtypeStruct((cells, size // (n_x * n_k), size), f32),
        in_specs=[hbm] * 3 + [smem] * 4 + [hbm] * 2,
        out_specs=vmem,
        scratch_shapes=[
            pltpu.VMEM(theta.shape, theta.dtype),
            pltpu.VMEM(target.shape, target.dtype),
            pltpu.VMEM(kernels.shape, f32),
            pltpu.VMEM(tabs.shape, tabs.dtype),
            pltpu.VMEM(wide.shape, f32),
            dma((5,)),
            pltpu.VMEM((cells, size, size), f32),
            pltpu.VMEM((n_z, cells, 2 * lanes), f32),
            pltpu.VMEM((n_z, n_k, cells, 2 * lanes), f32),
            pltpu.VMEM((n_k,) + kernels.shape, f32),
            pltpu.VMEM((n_k * here, rows, lanes), f32),
            pltpu.VMEM((n_k * here, rows, lanes), f32),
            pltpu.VMEM((n_k * here, 2 * grid, size), HALF),
            pltpu.VMEM((cells, tall, lanes), f32),
            pltpu.VMEM((ITERS, n_z, tall, lanes), LINK),
            pltpu.VMEM((ITERS, n_z, tall, lanes), LINK),
            pltpu.VMEM((ITERS, tall, lanes), LINK),
            pltpu.VMEM((ITERS, n_z, n_x, n_k, tall, lanes), LINK),
            dma((n_z, n_k)), dma((n_z, n_k)),
            dma((n_k,)), dma((n_k,)),
            dma((ITERS, n_z)), dma((ITERS, n_z)),
            dma((ITERS, n_z, n_x, n_k)), dma((ITERS, n_z, n_x, n_k)),
        ],
        compiler_params=pltpu.CompilerParams(
            collective_id=0, has_side_effects=True, vmem_limit_bytes=63 * 1024 * 1024
        ),
        cost_estimate=pl.CostEstimate(flops=10**9, bytes_accessed=10**7, transcendentals=10**6),
    )(theta, target, kernels, dose, inst_owner.reshape(-1), inst_local, inst_shift, jnp.asarray(tabs), jnp.asarray(wide))


def solution(mesh):
    in_specs = (
        P(("groups", "cells"), None, None),
        P(("groups", "cells"), None, None),
        P(None, "corners", "kern", None, None),
        P("corners"),
        P(("groups", "cells"), None),
        P(("groups", "cells")),
        P(("groups", "cells")),
    )
    out_specs = P(("groups", "cells"), ("corners", "kern"), None)
    return jax.shard_map(
        per_device, mesh=mesh, in_specs=in_specs, out_specs=out_specs, check_vma=False
    )
```

time: 501 us -> 37.4 us (0.07)
  matrix products: 211 us -> 0 us
  waiting for transfers between devices: 115 us -> 0 us
  local copies, waits for them, and re-layouts: 69.9 us -> 1.57 us
  blocking collectives: 58.2 us -> 0 us
  Pallas kernels: 0 us -> 35 us
  between operations: 15.1 us -> 0.66 us
  starting transfers between devices: 13.5 us -> 0 us
  other arithmetic: 11.2 us -> 0 us
    dot_general x414 -> x0, matrix products: 211 us -> none  [the longest x48 57.2 us: add_kernel(): jnp.einsum('xf,tfy->txy', inv_imag, half_imag, precision=hp)]
    unnamed x6 -> x0, waiting for transfers between devices: 63.5 us -> none
    all_to_all x2 -> x0, blocking collectives: 35.8 us -> none  [per_device(): lax.all_to_all(slot_grads, 'cells', split_axis=0, concat_axis=0, tiled=True)]
    pallas_call x0 -> x1, Pallas kernels: none -> 35 us  [per_device(): pl.pallas_call(functools.partial(body, (n_z, n_x, n_k, count, grid), plac...]
    psum x2 -> x0, waiting for transfers between devices: 32.6 us -> none  [per_device(): lax.psum(partial_image.astype(jnp.bfloat16), 'kern').astype(jnp.float32)]
    all_to_all x3 -> x0, waiting for transfers between devices: 18.4 us -> none  [the longest x2 15.4 us: per_device(): lax.all_to_all(outgoing, 'cells', split_axis=0, concat_axis=0, tiled=True)]
    dynamic_update_slice x48 -> x0, local copies, waits for them, and re-layouts: 18.1 us -> none  [intensity(): result, unused = lax.scan(add_kernel, start, (kern_real, kern_imag))]
    mul x48 -> x0, local copies, waits for them, and re-layouts: 17.9 us -> none  [add_kernel(): resp_real = pair[0] * spec_real - pair[1] * spec_imag]
  transfers between devices with their start and end apart: 7 -> 0, of which waited for: 7 -> 0; matrix products, arithmetic and copies ran while one was open for 1% -> 0% of each run, Pallas kernels for 0% -> 0%
where the time goes in v1:
time: 37.4 us; the launch traced here: 37.2 us
  Pallas kernels  35 us (94%)
  local copies, waits for them, and re-layouts  1.57 us (4%)
  between operations  0.66 us (2%)
    pallas_call x1, Pallas kernels, per_device(): pl.pallas_call(functools.partial(body, (n_z, n_x, n_k, count, grid), plac...  35 us
    unnamed x1, local copies, waits for them, and re-layouts  1.57 us

profile of v1, /device:TPU:0, one launch (start us, length us, event | category | flops | bytes accessed | tf_op | source)
XLA Modules:
  0.0 37.2 jit_solution(467496772984882750)
XLA Ops:
  0.7 35.0 %shard_map.91 = f32[8,32,128]{2,1,0:T(8,128)} custom-call(f32[8,128,128]{2,1,0:T(8,128)} %theta_hbm.1, bf16[2,128,128]{2,1,0:T(8,128)(2,1)} %target_hbm.1, f32[840,35]{1,0:T(8,128)} %bitcast.2, f32[1]{0:T(128)S(6)} %copy.11.dose, s32[16]{0:T(128)} %bitcast.3, s32[16]{0:T(128)} %local.1, s32[16]{0:T(128)} %shift.1, bf16[2096,128]{1,0:T(8,128)(2,1)} %constant.4.clone.tabs_hbm, ...), custom_call_target="tpu_custom_call" | custom-call | flops 1000000000 | bytes 10000000 | tf_op jit(solution)/shard_map/pallas_call | solution.py:347
  35.6 1.6 %copy.12 = f32[8,32,128]{2,1,0:T(8,128)} copy(f32[8,32,128]{2,1,0:T(8,128)} %shard_map.91) | data formatting | bytes 262144

commit v2 on v1

--- a/solution.py
+++ b/solution.py
@@ -98,7 +98,7 @@
 
 
 def body(sizes, places, theta_hbm, target_hbm, kernels_hbm, dose, owner, local, shift, tabs_hbm, wide_hbm, out,
-         theta, target, kernels, tabs, wide, loads, params, wsend, wrecv, kin, krr, kii, near, spectra, psend, precv, gsend, grecv,
+         theta, target, kernels, tabs, wide, loads, params, slope, wsend, wrecv, kin, krr, kii, near, spectra, psend, precv, gsend, grecv,
          ws, wr, ks, kr, ps, pr, gs, gr):
     n_z, n_x, n_k, count, grid = sizes
     cells, size = theta.shape[0], theta.shape[1]
@@ -190,14 +190,19 @@
         return jnp.concatenate([jnp.where(block == b, value, 0.0) for b in range(blocks)], 0)
 
     first_lane = lax.broadcasted_iota(jnp.int32, (size, lanes), 1)
+    pair = math.gcd(2, cells)
     centre = jnp.where((first_lane % (2 * half) == 0) & (first_lane < 2 * half * blocks), float(size), 0.0)
 
     def cell_spectra(source):
+        right = []
         for c in range(cells):
-            mask = jax.nn.sigmoid(source[c]).astype(HALF)
-            right = 2.0 * dot(mask, table("fy")) - centre
-            both = dot(table("fl"), right)
-            spectra[c] = gather_blocks(both[:rows]) + packed_times_i(gather_blocks(both[rows:]))
+            squash = jax.nn.sigmoid(source[c])
+            right.append((2.0 * dot(squash, table("fy")) - centre).astype(HALF))
+        for c in range(0, cells, pair):
+            wider = dot(table("fl"), jnp.concatenate(right[c : c + pair], 1))
+            for j in range(pair):
+                both = wider[:, j * lanes : (j + 1) * lanes]
+                spectra[c + j] = gather_blocks(both[:rows]) + packed_times_i(gather_blocks(both[rows:]))
 
     def spread(source, base):
         for part, wider in ((0, krr), (1, kii)):
@@ -222,6 +227,7 @@
         copy.wait_recv()
 
     chunk = math.gcd(12, here * n_k)
+    pair_k = math.gcd(2, chunk)
     steps = here * n_k // chunk
     wanted = target[k].astype(jnp.float32)
     dose_now = dose[0]
@@ -260,29 +266,38 @@
             for j in range(chunk):
                 at_k = step * chunk + j
                 resp.append((krr[at_k] * spec + kii[at_k] * turned_spec).astype(HALF))
-            half = dot(jnp.concatenate(resp, 0), table("gy")).astype(HALF)
-            for j in range(chunk):
-                one = half[j * rows : (j + 1) * rows]
-                stacked = jnp.concatenate([one[:, :size], one[:, size:]], 0)
+            wave = dot(jnp.concatenate(resp, 0), table("gy")).astype(HALF)
+            for j in range(0, chunk, pair_k):
+                ones = [wave[i * rows : (i + 1) * rows] for i in range(j, j + pair_k)]
+                stacked = jnp.concatenate(
+                    [
+                        jnp.concatenate([one[:, :size] for one in ones], 1),
+                        jnp.concatenate([one[:, size:] for one in ones], 1),
+                    ],
+                    0,
+                )
                 both = dot(table("gl"), stacked)
-                near[step * chunk + j] = both.astype(HALF)
+                near[(step * chunk + j) // pair_k] = both.astype(HALF)
                 image += both[:grid] * both[:grid] + both[grid:] * both[grid:]
             return image
 
-        image = lax.fori_loop(0, steps, forward, jnp.zeros((grid, size), jnp.float32))
+        image = lax.fori_loop(0, steps, forward, jnp.zeros((grid, pair_k * size), jnp.float32))
+        image = sum(image[:, j * size : (j + 1) * size] for j in range(pair_k))
         image = jnp.dot(wide[...], image, precision=lax.Precision.HIGHEST, preferred_element_type=jnp.float32)
         resist = jax.nn.sigmoid(STEEP * (dose_now * image - 1.0))
         pressure = (4.0 * STEEP) * dose_now * (resist - wanted) * resist * (1.0 - resist)
         pressure = dot(table("wt"), pressure)
-        pressure = jnp.concatenate([pressure, pressure], 0)
+        pressure = jnp.concatenate([jnp.concatenate([pressure] * pair_k, 1)] * 2, 0)
 
         def backward(step, sums):
             first, second = sums
             halves = []
-            for j in range(chunk):
-                both = near[step * chunk + j].astype(jnp.float32) * pressure
+            for j in range(0, chunk, pair_k):
+                both = near[(step * chunk + j) // pair_k].astype(jnp.float32) * pressure
                 left = dot(table("glt"), both).astype(HALF)
-                halves.append(jnp.concatenate([left[:rows], left[rows:]], 1))
+                for i in range(pair_k):
+                    one = left[:, i * size : (i + 1) * size]
+                    halves.append(jnp.concatenate([one[:rows], one[rows:]], 1))
             right = dot(jnp.concatenate(halves, 0), table("gyt"))
             for j in range(chunk):
                 at_k = step * chunk + j
@@ -302,6 +317,9 @@
         for a, c, b in others:
             gcopies[a, c, b] = send(gsend.at[it], grecv.at[it, a, c, b], gs.at[it, a, c, b], gr.at[it, a, c, b], at(a, b, c))
         flying += list(gcopies.values())
+        for c in range(cells):
+            squash = jax.nn.sigmoid(source[c])
+            slope[c] = 2.0 * squash * (1.0 - squash)
         sums = [jnp.zeros((tall, lanes), jnp.float32) for c in range(cells)]
         for a, b in [(0, 0)] + zk:
             for c in range(n_x):
@@ -314,14 +332,20 @@
                 w = wrecv[a, b, c : c + 1]
                 sums[c] += w[:, :lanes] * tile - w[:, lanes:] * turned
         right = dot(jnp.concatenate([part_blocks(one) for one in sums], 0), table("fyi")).astype(HALF)
-        for c in range(cells):
-            one = right[c * rows : (c + 1) * rows]
-            plane = dot(table("flt"), jnp.concatenate([one[:, :size], one[:, size:]], 0))
-            now = source[c]
-            squash = jax.nn.sigmoid(now)
-            grad = 2.0 * plane * squash * (1.0 - squash)
-            square = jnp.sum(jnp.sum(grad * grad, axis=0, keepdims=True), axis=1, keepdims=True)
-            params[c] = now - grad * (LR * lax.rsqrt(square / (size * size) + EPS))
+        for c in range(0, cells, pair):
+            ones = [right[i * rows : (i + 1) * rows] for i in range(c, c + pair)]
+            stacked = jnp.concatenate(
+                [
+                    jnp.concatenate([one[:, :size] for one in ones], 1),
+                    jnp.concatenate([one[:, size:] for one in ones], 1),
+                ],
+                0,
+            )
+            planes = dot(table("flt"), stacked)
+            for j in range(pair):
+                grad = planes[:, j * size : (j + 1) * size] * slope[c + j]
+                square = jnp.sum(jnp.sum(grad * grad, axis=0, keepdims=True), axis=1, keepdims=True)
+                params[c + j] = source[c + j] - grad * (LR * lax.rsqrt(square / (size * size) + EPS))
     band = out.shape[1]
     start = pl.multiple_of((x * n_k + k) * band, band)
     out[...] = params[:, pl.ds(start, band), :]
@@ -341,6 +365,7 @@
     rows = blocks * tall
     places, tabs, wide, grid = tables(size, count, mid)
     kernels = kernels.reshape(2 * here * count, count)
+    pair_k = math.gcd(2, n_k * here)
     f32, dma = jnp.float32, pltpu.SemaphoreType.DMA
     hbm = pl.BlockSpec(memory_space=pltpu.HBM)
     vmem, smem = pl.BlockSpec(memory_space=pltpu.VMEM), pl.BlockSpec(memory_space=pltpu.SMEM)
@@ -357,12 +382,13 @@
             pltpu.VMEM(wide.shape, f32),
             dma((5,)),
             pltpu.VMEM((cells, size, size), f32),
+            pltpu.VMEM((cells, size, size), f32),
             pltpu.VMEM((n_z, cells, 2 * lanes), f32),
             pltpu.VMEM((n_z, n_k, cells, 2 * lanes), f32),
             pltpu.VMEM((n_k,) + kernels.shape, f32),
             pltpu.VMEM((n_k * here, rows, lanes), f32),
             pltpu.VMEM((n_k * here, rows, lanes), f32),
-            pltpu.VMEM((n_k * here, 2 * grid, size), HALF),
+            pltpu.VMEM((n_k * here // pair_k, 2 * grid, pair_k * size), HALF),
             pltpu.VMEM((cells, tall, lanes), f32),
             pltpu.VMEM((ITERS, n_z, tall, lanes), LINK),
             pltpu.VMEM((ITERS, n_z, tall, lanes), LINK),

time: 37.4 us -> 36.8 us (0.984)
  Pallas kernels: 35 us -> 34.4 us
    pallas_call x1, Pallas kernels: 35 us -> 34.4 us  [per_device(): pl.pallas_call(functools.partial(body, (n_z, n_x, n_k, count, grid), plac...]
where the time goes in v2:
time: 36.8 us; the launch traced here: 36.6 us
  Pallas kernels  34.4 us (93%)
  local copies, waits for them, and re-layouts  1.57 us (4%)
  between operations  0.66 us (2%)
    pallas_call x1, Pallas kernels, per_device(): pl.pallas_call(functools.partial(body, (n_z, n_x, n_k, count, grid), plac...  34.4 us
    unnamed x1, local copies, waits for them, and re-layouts  1.57 us

profile of v2, /device:TPU:0, one launch (start us, length us, event | category | flops | bytes accessed | tf_op | source)
XLA Modules:
  0.0 36.6 jit_solution(6687252125265358945)
XLA Ops:
  0.7 34.4 %shard_map.91 = f32[8,32,128]{2,1,0:T(8,128)} custom-call(f32[8,128,128]{2,1,0:T(8,128)} %theta_hbm.1, bf16[2,128,128]{2,1,0:T(8,128)(2,1)} %target_hbm.1, f32[840,35]{1,0:T(8,128)} %bitcast.2, f32[1]{0:T(128)S(6)} %copy.11.dose, s32[16]{0:T(128)} %bitcast.3, s32[16]{0:T(128)} %local.1, s32[16]{0:T(128)} %shift.1, bf16[2096,128]{1,0:T(8,128)(2,1)} %constant.4.clone.tabs_hbm, ...), custom_call_target="tpu_custom_call" | custom-call | flops 1000000000 | bytes 10000000 | tf_op jit(solution)/shard_map/pallas_call | solution.py:372
  35.1 1.6 %copy.12 = f32[8,32,128]{2,1,0:T(8,128)} copy(f32[8,32,128]{2,1,0:T(8,128)} %shard_map.91) | data formatting | bytes 262144

commit v3 on v2

--- a/solution.py
+++ b/solution.py
@@ -78,7 +78,8 @@
     wide = np.cos(2.0 * math.pi * band[:, None, None] * gap[None]).sum(0) / grid
     if grid == size:
         wide = np.eye(size)
-    parts = dict(fy=fy, fl=fl, fyi=fyi, flt=flt, gy=gy, gyt=gy.T, gl=gl, glt=gl.T, wt=wide.T, flip=flip, expand=expand, fold=fold)
+    wide_hi = wide.astype(HALF).astype(np.float64)
+    parts = dict(fy=fy, fl=fl, fyi=fyi, flt=flt, gy=gy, gyt=gy.T, gl=gl, glt=gl.T, wide=np.concatenate([wide_hi, wide - wide_hi, wide_hi], 1), wt=wide.T, flip=flip, expand=expand, fold=fold)
     places, stack, top = {}, [], 0
     for name, t in parts.items():
         places[name] = []
@@ -90,15 +91,15 @@
             padded[: piece.shape[0], : piece.shape[1]] = piece
             stack.append(padded)
             top += tall
-    return places, np.concatenate(stack, 0).astype(HALF), wide.astype(np.float32), grid
+    return places, np.concatenate(stack, 0).astype(HALF), grid
 
 
 def dot(a, b):
     return jnp.dot(a.astype(HALF), b.astype(HALF), preferred_element_type=jnp.float32)
 
 
-def body(sizes, places, theta_hbm, target_hbm, kernels_hbm, dose, owner, local, shift, tabs_hbm, wide_hbm, out,
-         theta, target, kernels, tabs, wide, loads, params, slope, wsend, wrecv, kin, krr, kii, near, spectra, psend, precv, gsend, grecv,
+def body(sizes, places, theta_hbm, target_hbm, kernels_hbm, dose, owner, local, shift, tabs_hbm, out,
+         theta, target, kernels, tabs, loads, params, slope, wsend, wrecv, kin, krr, kii, near, spectra, psend, precv, gsend, grecv,
          ws, wr, ks, kr, ps, pr, gs, gr):
     n_z, n_x, n_k, count, grid = sizes
     cells, size = theta.shape[0], theta.shape[1]
@@ -126,7 +127,7 @@
         return pieces[0] if len(pieces) == 1 else jnp.concatenate(pieces, 1)
 
     local_copies = []
-    pairs = [(theta_hbm, theta), (tabs_hbm, tabs), (kernels_hbm, kernels), (target_hbm, target), (wide_hbm, wide)]
+    pairs = [(theta_hbm, theta), (tabs_hbm, tabs), (kernels_hbm, kernels), (target_hbm, target)]
     for j, (src, dst) in enumerate(pairs):
         copy = pltpu.make_async_copy(src, dst, loads.at[j])
         copy.start()
@@ -160,13 +161,13 @@
 
     pl.semaphore_wait(barrier, len(others))
     flying = []
-    wcopies, kcopies = [], []
-    for a, b in zk:
-        wcopies.append(send(wsend.at[lax.rem(z + a, n_z)], wrecv.at[a, b], ws.at[a, b], wr.at[a, b], at(a, b)))
+    wcopies, kcopies = {}, []
+    for a, b in sorted(zk, key=lambda ab: ab[1]):
+        wcopies[a, b] = (send(wsend.at[lax.rem(z + a, n_z)], wrecv.at[a, b], ws.at[a, b], wr.at[a, b], at(a, b)))
     for b in range(1, n_k):
         kcopies.append(send(kernels_hbm, kin.at[b], ks.at[b], kr.at[b], at(0, b)))
     wrecv[0, 0] = wsend[z]
-    flying += wcopies + kcopies
+    flying += list(wcopies.values()) + kcopies
 
     lane = lax.broadcasted_iota(jnp.int32, (rows, lanes), 1)
     sign = jnp.where(lane < mid, -1.0, 1.0)
@@ -223,10 +224,10 @@
     for copy in local_copies[2:]:
         copy.wait()
     spread(kernels, 0)
-    for copy in wcopies:
-        copy.wait_recv()
-
-    chunk = math.gcd(12, here * n_k)
+    for a in range(1, n_z):
+        wcopies[a, 0].wait_recv()
+
+    chunk = math.gcd(6, here * n_k)
     pair_k = math.gcd(2, chunk)
     steps = here * n_k // chunk
     wanted = target[k].astype(jnp.float32)
@@ -236,26 +237,28 @@
         source = theta if it == 0 else params
         if it > 0:
             cell_spectra(source)
-        totals = [jnp.zeros((tall, lanes), jnp.float32) for a in range(n_z)]
-        for c in range(cells):
-            value = spectra[c]
-            turned = packed_times_i(value)
-            for a in range(n_z):
+        values = [spectra[c] for c in range(cells)]
+        turned = [packed_times_i(value) for value in values]
+        pcopies = {}
+        spec = None
+        for a in list(range(n_z - 1, -1, -1)):
+            total = jnp.zeros((tall, lanes), jnp.float32)
+            for c in range(cells):
                 w = wrecv[a, 0, c : c + 1]
-                totals[a] += w[:, :lanes] * value + w[:, lanes:] * turned
-        pcopies = []
-        for a in range(1, n_z):
-            psend[it, a] = totals[a].astype(LINK)
-            pcopies.append(send(psend.at[it, a], precv.at[it, a], ps.at[it, a], pr.at[it, a],
-                                {"cells": lax.rem(z - a + n_z, n_z)}))
-        flying += pcopies
-        spec = totals[0]
+                total += w[:, :lanes] * values[c] + w[:, lanes:] * turned[c]
+            if a == 0:
+                spec = total
+            else:
+                psend[it, a] = total.astype(LINK)
+                pcopies[a] = send(psend.at[it, a], precv.at[it, a], ps.at[it, a], pr.at[it, a],
+                                  {"cells": lax.rem(z - a + n_z, n_z)})
+        flying += list(pcopies.values())
         if it == 0:
             for b, copy in zip(range(1, n_k), kcopies):
                 copy.wait_recv()
                 spread(kin.at[b], b * here)
         for a in range(1, n_z):
-            pcopies[a - 1].wait_recv()
+            pcopies[a].wait_recv()
             spec += precv[it, a].astype(jnp.float32)
         spec = part_blocks(spec).astype(HALF)
         spec = dot(jnp.concatenate([spec, dot(table("flip"), spec).astype(HALF)], 1), table("expand"))
@@ -281,9 +284,12 @@
                 image += both[:grid] * both[:grid] + both[grid:] * both[grid:]
             return image
 
-        image = lax.fori_loop(0, steps, forward, jnp.zeros((grid, pair_k * size), jnp.float32))
+        image = jnp.zeros((grid, pair_k * size), jnp.float32)
+        for step in range(steps):
+            image = forward(step, image)
         image = sum(image[:, j * size : (j + 1) * size] for j in range(pair_k))
-        image = jnp.dot(wide[...], image, precision=lax.Precision.HIGHEST, preferred_element_type=jnp.float32)
+        coarse = image.astype(HALF).astype(jnp.float32)
+        image = dot(table("wide"), jnp.concatenate([coarse, coarse, image - coarse], 0))
         resist = jax.nn.sigmoid(STEEP * (dose_now * image - 1.0))
         pressure = (4.0 * STEEP) * dose_now * (resist - wanted) * resist * (1.0 - resist)
         pressure = dot(table("wt"), pressure)
@@ -307,19 +313,25 @@
             return first, second
 
         zero = jnp.zeros((rows, lanes), jnp.float32)
-        first, second = lax.fori_loop(0, steps, backward, (zero, zero))
+        first, second = zero, zero
+        for step in range(steps):
+            first, second = backward(step, (first, second))
         tile = first - times_i(second)
         tile = tile.astype(HALF)
         tile = dot(jnp.concatenate([tile, dot(table("flip"), tile).astype(HALF)], 1), table("fold"))
         tile = gather_blocks(tile)
         gsend[it] = tile.astype(LINK)
         gcopies = {}
-        for a, c, b in others:
+        for a, c, b in sorted(others, key=lambda o: (o[0] == 0, -o[0])):
             gcopies[a, c, b] = send(gsend.at[it], grecv.at[it, a, c, b], gs.at[it, a, c, b], gr.at[it, a, c, b], at(a, b, c))
         flying += list(gcopies.values())
         for c in range(cells):
             squash = jax.nn.sigmoid(source[c])
             slope[c] = 2.0 * squash * (1.0 - squash)
+        if it == 0:
+            for a, b in zk:
+                if b > 0:
+                    wcopies[a, b].wait_recv()
         sums = [jnp.zeros((tall, lanes), jnp.float32) for c in range(cells)]
         for a, b in [(0, 0)] + zk:
             for c in range(n_x):
@@ -363,7 +375,7 @@
     lanes = 2 * mid
     half, blocks, share, tall = layout(count, lanes)
     rows = blocks * tall
-    places, tabs, wide, grid = tables(size, count, mid)
+    places, tabs, grid = tables(size, count, mid)
     kernels = kernels.reshape(2 * here * count, count)
     pair_k = math.gcd(2, n_k * here)
     f32, dma = jnp.float32, pltpu.SemaphoreType.DMA
@@ -372,15 +384,14 @@
     return pl.pallas_call(
         functools.partial(body, (n_z, n_x, n_k, count, grid), places),
         out_shape=jax.ShapeDtypeStruct((cells, size // (n_x * n_k), size), f32),
-        in_specs=[hbm] * 3 + [smem] * 4 + [hbm] * 2,
+        in_specs=[hbm] * 3 + [smem] * 4 + [hbm],
         out_specs=vmem,
         scratch_shapes=[
             pltpu.VMEM(theta.shape, theta.dtype),
             pltpu.VMEM(target.shape, target.dtype),
             pltpu.VMEM(kernels.shape, f32),
             pltpu.VMEM(tabs.shape, tabs.dtype),
-            pltpu.VMEM(wide.shape, f32),
-            dma((5,)),
+            dma((4,)),
             pltpu.VMEM((cells, size, size), f32),
             pltpu.VMEM((cells, size, size), f32),
             pltpu.VMEM((n_z, cells, 2 * lanes), f32),
@@ -403,7 +414,7 @@
             collective_id=0, has_side_effects=True, vmem_limit_bytes=63 * 1024 * 1024
         ),
         cost_estimate=pl.CostEstimate(flops=10**9, bytes_accessed=10**7, transcendentals=10**6),
-    )(theta, target, kernels, dose, inst_owner.reshape(-1), inst_local, inst_shift, jnp.asarray(tabs), jnp.asarray(wide))
+    )(theta, target, kernels, dose, inst_owner.reshape(-1), inst_local, inst_shift, jnp.asarray(tabs))
 
 
 def solution(mesh):

time: 36.8 us -> 36.8 us (level)
  no operation moved by 1% of the time
where the time goes in v3:
time: 36.8 us; the launch traced here: 36.6 us
  Pallas kernels  34.4 us (93%)
  local copies, waits for them, and re-layouts  1.57 us (4%)
  between operations  0.66 us (2%)
    pallas_call x1, Pallas kernels, per_device(): pl.pallas_call(functools.partial(body, (n_z, n_x, n_k, count, grid), plac...  34.4 us
    unnamed x1, local copies, waits for them, and re-layouts  1.57 us

profile of v3, /device:TPU:0, one launch (start us, length us, event | category | flops | bytes accessed | tf_op | source)
XLA Modules:
  0.0 36.6 jit_solution(1215678262441580552)
XLA Ops:
  0.7 34.4 %shard_map.82 = f32[8,32,128]{2,1,0:T(8,128)} custom-call(f32[8,128,128]{2,1,0:T(8,128)} %theta_hbm.1, bf16[2,128,128]{2,1,0:T(8,128)(2,1)} %target_hbm.1, f32[840,35]{1,0:T(8,128)} %bitcast.2, f32[1]{0:T(128)S(6)} %copy.10.dose, s32[16]{0:T(128)} %bitcast.3, s32[16]{0:T(128)} %local.1, s32[16]{0:T(128)} %shift.1, bf16[2352,128]{1,0:T(8,128)(2,1)} %constant.2.clone.tabs_hbm), custom_call_target="tpu_custom_call" | custom-call | flops 1000000000 | bytes 10000000 | tf_op jit(solution)/shard_map/pallas_call | solution.py:384
  35.1 1.6 %copy.11 = f32[8,32,128]{2,1,0:T(8,128)} copy(f32[8,32,128]{2,1,0:T(8,128)} %shard_map.82) | data formatting | bytes 262144
